TPU v7x, 32 devices: a whole 2x2x4 slice. The times are simulated.
32 devices in a mesh: batch: 8 (over y, x, core), lib: 4 (over z).
Axes of the slice: x: 2, y: 2, z: 4, core: 2. Of those that a mesh axis runs over, the one named last changes fastest.
Arguments:
- skip_features: bfloat16 [64, 1024, 320], P(('batch', 'lib')), may hold values from -6 to 6
- cached_deep_features: bfloat16 [64, 1024, 640], P('lib', 'batch'), may hold values from -6 to 6
- target_position: int32 [4, 16], P('lib'), may hold values from 0 to 15, each once within a row
- request_adapter: int32 [64], P(('batch', 'lib')), may hold values from 0 to 15
- library_adapter: int32 [16], P('lib'), may hold values from 0 to 15, each once
- adapter_down_weight: bfloat16 [16, 64, 960], P('lib'), may hold values from -0.1875 to 0.1875
- adapter_up_weight: bfloat16 [16, 64, 320], P('lib'), may hold values from -0.75 to 0.75
- kernel_weight: bfloat16 [3, 3, 960, 320], replicated, may hold values from -0.0625 to 0.0625
- shortcut_matrix: bfloat16 [960, 320], replicated, may hold values from -0.1875 to 0.1875
- group_norm_gain: float32 [960], replicated, may hold values from 0.5 to 1.5
- group_norm_offset: float32 [960], replicated, may hold values from -1.8 to 1.8
- output_bias: float32 [320], replicated, may hold values from -1.8 to 1.8
Outputs:
- block_out: bfloat16 [64, 1024, 320], P(('batch', 'lib'))
Inputs may be any that keep to these rules, and one draw needn't show every extreme that they name: Each row of target_position names every one of its 16 slots once. `request_adapter`: ids of adapters in the library. `library_adapter`: every adapter id is held in exactly one library slot.
All inputs are finite; a program needn't handle non-finite values.
Results may differ from a plain program's by a relative error of at most 0.0045.
Values may be sent and summed in bfloat16 or wider, within the bound.
A program may use at most 128 MiB of HBM per device.

v0:
```python
import jax
import jax.numpy as jnp
from jax import lax
from jax.sharding import PartitionSpec as P

DEEP = 640
GROUPS = 32
ROWS = 32
LAT_W = 32


def norm_silu(joined, group_norm_gain, group_norm_offset):
    count = joined.shape[0]
    places = joined.shape[1]
    width = joined.shape[2]
    values = joined.astype(jnp.float32).reshape(count, places, GROUPS, width // GROUPS)
    center = jnp.mean(values, axis=(1, 3), keepdims=True)
    spread = jnp.mean((values - center) ** 2, axis=(1, 3), keepdims=True)
    scaled = ((values - center) / jnp.sqrt(spread + 1e-05)).reshape(
        count, places, width
    ) * group_norm_gain + group_norm_offset
    return jax.nn.silu(scaled).astype(jnp.bfloat16)


def local(
    skip_features,
    cached_deep_features,
    target_position,
    request_adapter,
    library_adapter,
    adapter_down_weight,
    adapter_up_weight,
    kernel_weight,
    shortcut_matrix,
    group_norm_gain,
    group_norm_offset,
    output_bias,
):
    batch_count = lax.axis_size("batch")
    per_device = skip_features.shape[0]
    places = skip_features.shape[1]
    column = target_position.shape[1]
    width = kernel_weight.shape[2]
    outputs = kernel_weight.shape[3]
    placing = target_position[0]
    inverse = jnp.zeros((column,), jnp.int32).at[placing].set(jnp.arange(column, dtype=jnp.int32))
    order = inverse.reshape(batch_count, per_device).T
    outgoing = cached_deep_features[order]
    arrived = lax.all_to_all(outgoing, "batch", split_axis=1, concat_axis=1, tiled=True)
    deep = arrived.reshape(per_device, places, DEEP)
    down_portion = lax.all_gather(adapter_down_weight, "lib", axis=0, tiled=True)
    up_portion = lax.all_gather(adapter_up_weight, "lib", axis=0, tiled=True)
    id_piece = lax.all_gather(library_adapter, "lib", axis=0, tiled=True)
    picker = (request_adapter[:, None] == id_piece[None, :]).astype(jnp.bfloat16)
    down_sum = jnp.einsum("rk,kij->rij", picker, down_portion, preferred_element_type=jnp.float32)
    up_sum = jnp.einsum("rk,kij->rij", picker, up_portion, preferred_element_type=jnp.float32)
    down_sum, up_sum = (down_sum, up_sum)
    down_blocks = down_sum.astype(jnp.bfloat16)
    up_blocks = up_sum.astype(jnp.bfloat16)
    joined = jnp.concatenate([skip_features, deep], axis=2)
    normed = norm_silu(joined, group_norm_gain, group_norm_offset)
    padded = jnp.pad(
        normed.reshape(per_device, ROWS, LAT_W, width), ((0, 0), (1, 1), (1, 1), (0, 0))
    )
    conv = jnp.zeros((per_device * places, outputs), jnp.float32)
    for row_off in range(3):
        for col_off in range(3):
            window = padded[:, row_off : row_off + ROWS, col_off : col_off + LAT_W].reshape(
                per_device * places, width
            )
            conv = conv + jnp.dot(
                window, kernel_weight[row_off, col_off], preferred_element_type=jnp.float32
            )
    shortcut = jnp.dot(
        joined.reshape(per_device * places, width),
        shortcut_matrix,
        preferred_element_type=jnp.float32,
    )
    low = jnp.einsum(
        "rpc,rkc->rpk", normed, down_blocks, preferred_element_type=jnp.float32
    ).astype(jnp.bfloat16)
    delta = jnp.einsum("rpk,rko->rpo", low, up_blocks, preferred_element_type=jnp.float32)
    total = (shortcut + conv).reshape(per_device, places, outputs) + output_bias + delta
    return total.astype(jnp.bfloat16)


def solution(mesh):
    in_specs = (
        P(("batch", "lib"), None, None),
        P("lib", "batch", None),
        P("lib", None),
        P(("batch", "lib")),
        P("lib"),
        P("lib", None, None),
        P("lib", None, None),
        P(),
        P(),
        P(),
        P(),
        P(),
    )
    out_specs = P(("batch", "lib"), None, None)
    return jax.shard_map(local, mesh=mesh, in_specs=in_specs, out_specs=out_specs, check_vma=False)
```

profile of v0, /device:TPU:0, one launch (start us, length us, event | category | flops | bytes accessed | tf_op | source)
XLA Modules:
  0.0 148.1 jit_solution(5434966734072437644)
XLA Ops:
  6.5 0.8 fusion.48
  7.3 0.6 scatter_custom_fusion
  8.3 2.4 %gather_fusion = bf16[16,128,640]{2,1,0:T(8,128)(2,1)} fusion(bf16[16,128,640]{2,1,0:T(8,128)(2,1)S(1)} %copy-done, s32[1024]{0:T(1024)S(1)} %pad_clamp_fusion), kind=kCustom, calls=%fused_computation | custom fusion | bytes 5242944 | tf_op jit(solution)/shard_map/gather | solution.py:48
  10.7 3.6 %copy.34 = bf16[2,8,128,640]{3,2,0,1:T(8,128)(2,1)} copy(bf16[2,8,128,640]{3,2,1,0:T(8,128)(2,1)} %bitcast.86) | data formatting | bytes 5242880 | tf_op jit(solution)/shard_map/gather | solution.py:48
  14.3 5.3 %all-to-all-start = ((bf16[2,8,128,640]{3,2,0,1:T(8,128)(2,1)}), bf16[2,8,128,640]{3,2,0,1:T(8,128)(2,1)}, u32[]{:S(2)}, u32[]{:S(2)}) async-start(bf16[2,8,128,640]{3,2,0,1:T(8,128)(2,1)} %copy.34), calls=%async_computation | async-start | bytes 5242880 | tf_op jit(solution)/shard_map/all_to_all | solution.py:49
  19.6 0.7 all-gather.2.cloned.1.call-update
  20.3 1.6 %copy.49 = bf16[2,1024,320]{2,1,0:T(8,128)(2,1)} copy(bf16[2,1024,320]{1,2,0:T(8,128)(2,1)S(1)} %copy-done.9) | data formatting | bytes 2621440 | tf_op jit(solution)/shard_map/concatenate | solution.py:60
  21.9 0.6 dynamic-slice
  23.2 0.2 dynamic-update-slice
  23.4 9.2 %all-reduce.1 = s32[16]{0:T(128)S(1)} all-reduce(s32[16]{0:T(128)S(1)} %dynamic-update-slice), channel_id=1, replica_groups=mesh['batch'=8,'lib'=4] {'lib'}, use_global_device_ids=true, to_apply=%add.1 | all-reduce | flops 16 | bytes 128
  32.6 29.5 %all_gather.11 = bf16[16,64,320]{2,1,0:T(8,128)(2,1)S(1)} all-gather(bf16[4,64,320]{2,1,0:T(8,128)(2,1)S(1)} %copy-done.10), channel_id=1, replica_groups=mesh['batch'=8,'lib'=4] {'lib'}, dimensions={0}, use_global_device_ids=true | all-gather | bytes 819200 | tf_op jit(solution)/shard_map/all_gather | solution.py:52
  62.1 0.5 convolution_convert_fusion.1
  62.7 2.2 %copy.35 = bf16[2,8,128,640]{3,2,1,0:T(8,128)(2,1)S(1)} copy(bf16[2,8,128,640]{3,2,0,1:T(8,128)(2,1)} %all-to-all-done) | data formatting | bytes 5242880 | tf_op jit(solution)/shard_map/all_to_all | solution.py:49
  64.9 1.7 %convert_reduce_fusion = f32[2,960]{1,0:T(2,128)S(1)} fusion(bf16[2,1024,640]{2,1,0:T(8,128)(2,1)S(1)} %bitcast.72, bf16[2,1024,320]{2,1,0:T(8,128)(2,1)S(1)} %copy-done.2), kind=kLoop, calls=%fused_computation.3 | loop fusion | flops 9828480 | bytes 3939840 | tf_op jit(solution)/shard_map/reduce_sum | solution.py:17
  67.1 3.6 %fusion.2 = f32[2,960]{1,0:T(2,128)S(1)} fusion(f32[2,960]{1,0:T(2,128)S(1)} %sub.32, bf16[2,1024,640]{2,1,0:T(8,128)(2,1)S(1)} %bitcast.73, bf16[2,1024,320]{2,1,0:T(8,128)(2,1)} %copy.49), kind=kLoop, calls=%fused_computation.6 | loop fusion | flops 13760640 | bytes 3947520 | tf_op jit(solution)/shard_map/reduce_sum | solution.py:18
  71.1 6.8 %multiply_convert_fusion = bf16[2,1024,960]{2,1,0:T(8,128)(2,1)} fusion(f32[960]{0:T(1024)S(1)} %copy-done.11, f32[960]{0:T(1024)S(1)} %copy-done.12, f32[2,960]{1,0:T(2,128)S(1)} %div.50, f32[2,960]{1,0:T(2,128)S(1)} %sub.32, bf16[2,1024,640]{2,1,0:T(8,128)(2,1)S(1)} %bitcast.74, bf16[2,1024,320]{2,1,0:T(8,128)(2,1)} %copy.49), kind=kLoop, calls=%fused_computation.9 | loop fusion | flops 25559040 | bytes 7887360 | tf_op jit(solution)/shard_map/convert_element_type | solution.py:22
  77.9 5.6 %multiply_convert_fusion.1 = bf16[2,32,32,960]{3,2,1,0:T(8,128)(2,1)} fusion(bf16[2,32,32,640]{3,2,1,0:T(8,128)(2,1)S(1)} %bitcast.75, bf16[2,32,32,320]{3,2,1,0:T(8,128)(2,1)S(1)} %bitcast.77, f32[960]{0:T(1024)S(1)} %copy-done.11, f32[960]{0:T(1024)S(1)} %copy-done.12, f32[2,960]{1,0:T(2,128)S(1)} %div.50, f32[2,960]{1,0:T(2,128)S(1)} %sub.32), kind=kLoop, calls=%fused_computation.10 | loop fusion | flops 25559040 | bytes 7887360 | tf_op jit(solution)/shard_map/convert_element_type | solution.py:22
  83.5 22.2 %pad_slice_fusion = (bf16[2,32,32,960]{3,2,1,0:T(8,128)(2,1)S(1)}, bf16[2,32,32,960]{3,2,1,0:T(8,128)(2,1)}, bf16[2,32,32,960]{3,2,1,0:T(8,128)(2,1)}, bf16[2,32...) fusion(bf16[2,32,32,960]{3,2,1,0:T(8,128)(2,1)} %multiply_conve, ...), kind=kLoop, calls=%fused_computation.11 | loop fusion | bytes 35389440 | tf_op jit(solution)/shard_map/slice | solution.py:68
  105.8 4.1 %fusion.30 = f32[2048,320]{0,1:T(8,128)S(1)} fusion(bf16[2048,960]{1,0:T(8,128)(2,1)} %bitcast.88, bf16[3,3,960,320]{2,3,1,0:T(8,128)(2,1)} %param.19), kind=kOutput, calls=%fused_computation.51 | convolution fusion | flops 1258291200 | bytes 7471104 | tf_op jit(solution)/shard_map/dot_general | solution.py:71
  109.9 2.8 %convolution_add_fusion.6 = f32[2048,320]{0,1:T(8,128)S(1)} fusion(f32[2048,320]{0,1:T(8,128)S(1)} %fusion.30, bf16[2048,960]{1,0:T(8,128)(2,1)S(1)} %bitcast.84, bf16[3,3,960,320]{2,3,1,0:T(8,128)(2,1)} %param.19), kind=kOutput, calls=%fused_computation.32 | convolution fusion | flops 1258946560 | bytes 9830400 | tf_op jit(solution)/shard_map/dot_general | solution.py:71
  112.9 1.6 %convolution_add_fusion.5 = f32[2048,320]{0,1:T(8,128)S(1)} fusion(f32[2048,320]{0,1:T(8,128)S(1)} %convolution_add_fusion.6, bf16[2048,960]{1,0:T(8,128)(2,1)S(1)} %bitcast.83, bf16[3,3,960,320]{2,3,1,0:T(8,128)(2,1)S(1)} %bitcast.90), kind=kOutput, calls=%fused_computation.31 | convolution fusion | flops 1258946560 | bytes 10092544 | tf_op jit(solution)/shard_map/dot_general | solution.py:71
  114.5 0.6 copy-done.4
  115.1 1.6 %convolution_add_fusion.4 = f32[2048,320]{0,1:T(8,128)S(1)} fusion(f32[2048,320]{0,1:T(8,128)S(1)} %convolution_add_fusion.5, bf16[2048,960]{1,0:T(8,128)(2,1)S(1)} %bitcast.82, bf16[3,3,960,320]{2,3,1,0:T(8,128)(2,1)S(1)} %bitcast.90), kind=kOutput, calls=%fused_computation.30 | convolution fusion | flops 1258946560 | bytes 10092544 | tf_op jit(solution)/shard_map/dot_general | solution.py:71
  116.7 0.6 copy-done.8
  117.3 3.1 %fusion.24 = f32[2048,320]{0,1:T(8,128)} fusion(bf16[2048,960]{1,0:T(8,128)(2,1)S(1)} %bitcast.87, bf16[3,3,960,320]{2,3,1,0:T(8,128)(2,1)S(1)} %bitcast.90), kind=kOutput, calls=%fused_computation.45 | convolution fusion | flops 1258291200 | bytes 7471104 | tf_op jit(solution)/shard_map/dot_general | solution.py:71
  120.4 3.5 %fusion.12 = f32[2048,320]{0,1:T(8,128)S(1)} fusion(f32[2048,320]{0,1:T(8,128)} %fusion.24, f32[2048,320]{0,1:T(8,128)S(1)} %convolution_add_fusion.4, bf16[2048,960]{1,0:T(8,128)(2,1)S(1)} %bitcast.85, bf16[3,3,960,320]{2,3,1,0:T(8,128)(2,1)S(1)} %bitcast.90), kind=kOutput, calls=%fused_computation.26 | convolution fusion | flops 1259601920 | bytes 12713984 | tf_op jit(solution)/shard_map/dot_general | solution.py:71
  123.9 1.6 %convolution_add_fusion.3 = f32[2048,320]{0,1:T(8,128)S(1)} fusion(f32[2048,320]{0,1:T(8,128)S(1)} %fusion.12, bf16[2048,960]{1,0:T(8,128)(2,1)S(1)} %bitcast.81, bf16[3,3,960,320]{2,3,1,0:T(8,128)(2,1)S(1)} %bitcast.90), kind=kOutput, calls=%fused_computation.29 | convolution fusion | flops 1258946560 | bytes 10092544 | tf_op jit(solution)/shard_map/dot_general | solution.py:71
  125.5 1.6 %convolution_add_fusion.2 = f32[2048,320]{0,1:T(8,128)S(1)} fusion(f32[2048,320]{0,1:T(8,128)S(1)} %convolution_add_fusion.3, bf16[2048,960]{1,0:T(8,128)(2,1)S(1)} %bitcast.80, bf16[3,3,960,320]{2,3,1,0:T(8,128)(2,1)S(1)} %bitcast.90), kind=kOutput, calls=%fused_computation.28 | convolution fusion | flops 1258946560 | bytes 10092544 | tf_op jit(solution)/shard_map/dot_general | solution.py:71
  127.2 1.9 %convolution_add_fusion.1 = f32[2048,320]{0,1:T(8,128)S(1)} fusion(f32[2048,320]{0,1:T(8,128)S(1)} %convolution_add_fusion.2, bf16[2048,960]{1,0:T(8,128)(2,1)S(1)} %bitcast.79, bf16[3,3,960,320]{2,3,1,0:T(8,128)(2,1)S(1)} %bitcast.90), kind=kOutput, calls=%fused_computation.27 | convolution fusion | flops 1258946560 | bytes 10092544 | tf_op jit(solution)/shard_map/dot_general | solution.py:71
  129.1 3.3 %fusion.9 = f32[2048,320]{0,1:T(8,128)} fusion(f32[2048,320]{0,1:T(8,128)S(1)} %convolution_add_fusion.1, bf16[960,320]{0,1:T(8,128)(2,1)S(1)} %copy-done.15, bf16[2048,640]{1,0:T(8,128)(2,1)S(1)} %bitcast.76, bf16[2048,320]{1,0:T(8,128)(2,1)S(1)} %bitcast.78), kind=kOutput, calls=%fused_computation.24 | convolution fusion | flops 1266810880 | bytes 9789440 | tf_op jit(solution)/shard_map/dot_general | solution.py:74
  132.4 2.9 %fusion.17 = bf16[2,64,960]{2,0,1:T(2,128)(2,1)S(1)} fusion(bf16[16,64,960]{2,1,0:T(8,128)(2,1)} %all-gather.2.cloned.1.call-done, s32[16]{0:T(128)S(1)} %all-reduce.1, s32[2]{0:T(128)S(1)} %copy-done.14), kind=kOutput, calls=%fused_computation.39 | convolution fusion | flops 4055072 | bytes 2211912 | tf_op jit(solution)/shard_map/rk,kij->rij/dot_general | solution.py:55
  135.3 6.0 %fusion.14 = bf16[2,1024,320]{1,2,0:T(8,128)(2,1)} fusion(f32[40,2,8,1024]{3,2,1,0:T(8,128)} %bitcast.91, f32[320]{0:T(512)S(1)} %copy-done.13, bf16[2,1024,960]{2,1,0:T(8,128)(2,1)} %multiply_convert_fusion, bf16[2,64,960]{2,0,1:T(2,128)(2,1)S(1)} %fusion.17, bf16[2,64,320]{2,0,1:T(2,128)(2,1)S(1)} %convolution_convert_fusion.1), kind=kOutput, calls=%fused_computation.35 | convolution fusion | flops 337641472 | bytes 8193280 | tf_op jit(solution)/shard_map/rpk,rko->rpo/dot_general | solution.py:82
  (59 shorter events, 1.4 us)
Async XLA Ops:
  6.5 1.8 %copy-start = (bf16[16,128,640]{2,1,0:T(8,128)(2,1)S(1)}, bf16[16,128,640]{2,1,0:T(8,128)(2,1)}, u32[]{:S(2)}) copy-start(bf16[16,128,640]{2,1,0:T(8,128)(2,1)} %param.13) | copy-start | bytes 7864324
  14.3 6.1 %copy-start.9 = (bf16[2,1024,320]{1,2,0:T(8,128)(2,1)S(1)}, bf16[2,1024,320]{1,2,0:T(8,128)(2,1)}, u32[]{:S(2)}) copy-start(bf16[2,1024,320]{1,2,0:T(8,128)(2,1)} %param.12) | copy-start | bytes 3932164
  14.3 7.7 %copy-start.17 = (u32[32]{0:T(128)S(1)}, u32[32]{0:T(128)}, u32[]{:S(2)}) copy-start(u32[32]{0:T(128)} %constant.27) | copy-start | bytes 388
  14.3 8.9 %copy-start.16 = (s32[4]{0:T(128)S(1)}, s32[4]{0:T(128)}, u32[]{:S(2)}) copy-start(s32[4]{0:T(128)} %param.16) | copy-start | bytes 52
  14.3 18.3 %copy-start.10 = (bf16[4,64,320]{2,1,0:T(8,128)(2,1)S(1)}, bf16[4,64,320]{2,1,0:T(8,128)(2,1)}, u32[]{:S(2)}) copy-start(bf16[4,64,320]{2,1,0:T(8,128)(2,1)} %param.18) | copy-start | bytes 491524
  14.3 47.8 %copy-start.14 = (s32[2]{0:T(128)S(1)}, s32[2]{0:T(128)}, u32[]{:S(2)}) copy-start(s32[2]{0:T(128)} %param.15) | copy-start | bytes 28
  14.3 48.4 %all-to-all-start = ((bf16[2,8,128,640]{3,2,0,1:T(8,128)(2,1)}), bf16[2,8,128,640]{3,2,0,1:T(8,128)(2,1)}, u32[]{:S(2)}, u32[]{:S(2)}) async-start(bf16[2,8,128,640]{3,2,0,1:T(8,128)(2,1)} %copy.34), calls=%async_computation | async-start | bytes 5242880 | tf_op jit(solution)/shard_map/all_to_all | solution.py:49
  19.6 112.8 %all-gather.2.cloned.1.call-start = ((), (), s32[]{:S(2)}) async-start(), calls=%async_computation.1 | async-start | bytes 2621440 | tf_op jit(solution)/shard_map/all_gather | solution.py:51
  62.7 2.2 %copy-start.2 = (bf16[2,1024,320]{2,1,0:T(8,128)(2,1)S(1)}, bf16[2,1024,320]{2,1,0:T(8,128)(2,1)}, u32[]{:S(2)}) copy-start(bf16[2,1024,320]{2,1,0:T(8,128)(2,1)} %copy.49) | copy-start | bytes 3932164
  64.9 6.2 %copy-start.11 = (f32[960]{0:T(1024)S(1)}, f32[960]{0:T(1024)}, u32[]{:S(2)}) copy-start(f32[960]{0:T(1024)} %param.22) | copy-start | bytes 11524
  64.9 6.2 %copy-start.12 = (f32[960]{0:T(1024)S(1)}, f32[960]{0:T(1024)}, u32[]{:S(2)}) copy-start(f32[960]{0:T(1024)} %param.21) | copy-start | bytes 11524
  71.1 6.9 %copy-start.3 = (bf16[2,1024,320]{2,1,0:T(8,128)(2,1)S(1)}, bf16[2,1024,320]{2,1,0:T(8,128)(2,1)}, u32[]{:S(2)}) copy-start(bf16[2,1024,320]{2,1,0:T(8,128)(2,1)} %copy.49) | copy-start | bytes 3932164
  105.8 4.1 %copy-start.6 = (bf16[2,32,32,960]{3,2,1,0:T(8,128)(2,1)S(1)}, bf16[2,32,32,960]{3,2,1,0:T(8,128)(2,1)}, u32[]{:S(2)}) copy-start(bf16[2,32,32,960]{3,2,1,0:T(8,128)(2,1)} %get-tuple-element.6) | copy-start | bytes 11796484
  105.8 6.9 %slice-start = ((s8[5898240]{0:T(1024)(128)(4,1)}), s8[4194304]{0:T(1024)(128)(4,1)S(1)}, s32[]{:S(2)}) async-start(s8[5898240]{0:T(1024)(128)(4,1)} %bitcast.89), calls=%async_computation.2 | async-start | bytes 8388608
  109.9 2.9 %copy-start.5 = (bf16[2,32,32,960]{3,2,1,0:T(8,128)(2,1)S(1)}, bf16[2,32,32,960]{3,2,1,0:T(8,128)(2,1)}, u32[]{:S(2)}) copy-start(bf16[2,32,32,960]{3,2,1,0:T(8,128)(2,1)} %get-tuple-element.7) | copy-start | bytes 11796484
  109.9 3.0 %slice-start.1 = ((s8[5898240]{0:T(1024)(128)(4,1)}), s8[1703936]{0:T(1024)(128)(4,1)S(1)}, s32[]{:S(2)}) async-start(s8[5898240]{0:T(1024)(128)(4,1)} %bitcast.89), calls=%async_computation.3 | async-start | bytes 3407872
  112.9 2.2 %copy-start.4 = (bf16[2,32,32,960]{3,2,1,0:T(8,128)(2,1)S(1)}, bf16[2,32,32,960]{3,2,1,0:T(8,128)(2,1)}, u32[]{:S(2)}) copy-start(bf16[2,32,32,960]{3,2,1,0:T(8,128)(2,1)} %get-tuple-element.8) | copy-start | bytes 11796484
  115.1 2.2 %copy-start.8 = (bf16[2,32,32,960]{3,2,1,0:T(8,128)(2,1)S(1)}, bf16[2,32,32,960]{3,2,1,0:T(8,128)(2,1)}, u32[]{:S(2)}) copy-start(bf16[2,32,32,960]{3,2,1,0:T(8,128)(2,1)} %get-tuple-element.9) | copy-start | bytes 11796484
  117.3 3.1 %copy-start.7 = (bf16[2,1024,960]{2,1,0:T(8,128)(2,1)S(1)}, bf16[2,1024,960]{2,1,0:T(8,128)(2,1)}, u32[]{:S(2)}) copy-start(bf16[2,1024,960]{2,1,0:T(8,128)(2,1)} %multiply_convert_fusion) | copy-start | bytes 11796484
  127.2 1.9 %copy-start.15 = (bf16[960,320]{0,1:T(8,128)(2,1)S(1)}, bf16[960,320]{0,1:T(8,128)(2,1)}, u32[]{:S(2)}) copy-start(bf16[960,320]{0,1:T(8,128)(2,1)} %param.20) | copy-start | bytes 1843204
  129.1 6.2 %copy-start.13 = (f32[320]{0:T(512)S(1)}, f32[320]{0:T(512)}, u32[]{:S(2)}) copy-start(f32[320]{0:T(512)} %param.23) | copy-start | bytes 3844
  135.3 6.0 %copy-start.1 = (bf16[16,128,640]{2,1,0:T(8,128)(2,1)S(1)}, bf16[16,128,640]{2,1,0:T(8,128)(2,1)}, u32[]{:S(2)}) copy-start(bf16[16,128,640]{2,1,0:T(8,128)(2,1)} %param.13) | copy-start | bytes 7864324
Sparse Core Ops, SparseCore 0:
  22.0 60.5 all-gather.1
where the time goes:
time: 149 us; the launch traced here: 148 us
  blocking collectives  38.7 us (26%)
  local copies, waits for them, and re-layouts  35.9 us (24%)
  matrix products  34.4 us (23%)
  other arithmetic  18.8 us (13%)
  between operations  14.4 us (10%)
  starting transfers between devices  5.35 us (4%)
    all_gather x1, blocking collectives, local(): up_portion = lax.all_gather(adapter_up_weight, 'lib', axis=0, tiled=True)  29.5 us
    slice x1, local copies, waits for them, and re-layouts, local(): padded[:, row_off:row_off + ROWS, col_off:col_off + LAT_W]  22.2 us
    dot_general x9, matrix products, local(): jnp.dot(window, kernel_weight[row_off, col_off], preferred_element_type=j...  21.7 us
    convert_element_type x2, other arithmetic, norm_silu(): return jax.nn.silu(scaled).astype(jnp.bfloat16)  12.4 us
    unnamed x1, blocking collectives  9.15 us
    dot_general x1, matrix products, local(): jnp.einsum('rpk,rko->rpo', low, up_blocks, preferred_element_type=jnp.flo...  5.97 us
    gather x2, local copies, waits for them, and re-layouts, local(): outgoing = cached_deep_features[order]  5.97 us
    all_to_all x1, starting transfers between devices, local(): lax.all_to_all(outgoing, 'batch', split_axis=1, concat_axis=1, tiled=True)  5.31 us
  transfers between devices with their start and end apart: 2, of which 0 were waited for; matrix products, arithmetic and copies ran while one was open for 48% of the time, Pallas kernels for 0%

commit v1 on v0

--- a/solution.py
+++ b/solution.py
@@ -49,7 +49,18 @@
     arrived = lax.all_to_all(outgoing, "batch", split_axis=1, concat_axis=1, tiled=True)
     deep = arrived.reshape(per_device, places, DEEP)
     down_portion = lax.all_gather(adapter_down_weight, "lib", axis=0, tiled=True)
-    up_portion = lax.all_gather(adapter_up_weight, "lib", axis=0, tiled=True)
+    ways = lax.axis_size("lib")
+    up = [(d, (d + 1) % ways) for d in range(ways)]
+    down = [(d, (d - 1) % ways) for d in range(ways)]
+    earlier, later = ([adapter_up_weight], [adapter_up_weight])
+    for _ in range(ways // 2):
+        earlier.append(lax.ppermute(earlier[-1], "lib", up))
+    for _ in range((ways - 1) // 2):
+        later.append(lax.ppermute(later[-1], "lib", down))
+    line = jnp.concatenate([*earlier[::-1], *later[1:]], axis=0)
+    up_portion = jnp.roll(
+        line, (lax.axis_index("lib") - ways // 2) * adapter_up_weight.shape[0], axis=0
+    )
     id_piece = lax.all_gather(library_adapter, "lib", axis=0, tiled=True)
     picker = (request_adapter[:, None] == id_piece[None, :]).astype(jnp.bfloat16)
     down_sum = jnp.einsum("rk,kij->rij", picker, down_portion, preferred_element_type=jnp.float32)

time: 149 us -> 140 us (0.940)
  blocking collectives: 38.7 us -> 11.7 us
  waiting for transfers between devices: 0.68 us -> 10.5 us
  starting transfers between devices: 5.35 us -> 9.77 us
  local copies, waits for them, and re-layouts: 35.9 us -> 38.2 us
  other arithmetic: 18.8 us -> 20.5 us
    all_gather x1 -> x0, blocking collectives: 29.5 us -> none  [local(): up_portion = lax.all_gather(adapter_up_weight, 'lib', axis=0, tiled=True)]
    ppermute x0 -> x3, waiting for transfers between devices: none -> 5.65 us  [the longest x2 5.64 us: local(): earlier.append(lax.ppermute(earlier[-1], 'lib', up))]
    all_to_all x1, waiting for transfers between devices: 0.01 us -> 4.84 us  [local(): lax.all_to_all(outgoing, 'batch', split_axis=1, concat_axis=1, tiled=True)]
    ppermute x0 -> x3, starting transfers between devices: none -> 4.43 us  [the longest x2 2.34 us: local(): earlier.append(lax.ppermute(earlier[-1], 'lib', up))]
    unnamed x1, blocking collectives: 9.15 us -> 11.7 us
    concatenate x0 -> x1, local copies, waits for them, and re-layouts: none -> 1.97 us  [local(): jnp.roll(line, (lax.axis_index('lib') - ways // 2) * adapter_up_weight.sh...]
    reduce_sum x2, other arithmetic: 1.82 us -> 3.51 us  [norm_silu(): center = jnp.mean(values, axis=(1, 3), keepdims=True)]
  transfers between devices with their start and end apart: 2 -> 5, of which waited for: 0 -> 2; matrix products, arithmetic and copies ran while one was open for 48% -> 54% of each run, Pallas kernels for 0% -> 0%
where the time goes in v1:
time: 140 us; the launch traced here: 139 us
  local copies, waits for them, and re-layouts  38.2 us (27%)
  matrix products  34.2 us (24%)
  other arithmetic  20.5 us (15%)
  between operations  14.4 us (10%)
  blocking collectives  11.7 us (8%)
  waiting for transfers between devices  10.5 us (8%)
  starting transfers between devices  9.77 us (7%)
    slice x1, local copies, waits for them, and re-layouts, local(): padded[:, row_off:row_off + ROWS, col_off:col_off + LAT_W]  22.5 us
    dot_general x9, matrix products, local(): jnp.dot(window, kernel_weight[row_off, col_off], preferred_element_type=j...  21.7 us
    convert_element_type x2, other arithmetic, norm_silu(): return jax.nn.silu(scaled).astype(jnp.bfloat16)  12.4 us
    unnamed x1, blocking collectives  11.7 us
    gather x2, local copies, waits for them, and re-layouts, local(): outgoing = cached_deep_features[order]  6.01 us
    dot_general x1, matrix products, local(): jnp.einsum('rpk,rko->rpo', low, up_blocks, preferred_element_type=jnp.flo...  5.96 us
    ppermute x2, waiting for transfers between devices, local(): earlier.append(lax.ppermute(earlier[-1], 'lib', up))  5.64 us
    all_to_all x1, starting transfers between devices, local(): lax.all_to_all(outgoing, 'batch', split_axis=1, concat_axis=1, tiled=True)  5.3 us
  transfers between devices with their start and end apart: 5, of which 2 were waited for; matrix products, arithmetic and copies ran while one was open for 54% of the time, Pallas kernels for 0%

profile of v1, /device:TPU:0, one launch (start us, length us, event | category | flops | bytes accessed | tf_op | source)
XLA Modules:
  0.0 139.2 jit_solution(13230875354458626727)
XLA Ops:
  6.5 0.8 fusion.48
  7.3 0.6 scatter_custom_fusion
  8.3 2.4 %gather_fusion = bf16[16,128,640]{2,1,0:T(8,128)(2,1)} fusion(bf16[16,128,640]{2,1,0:T(8,128)(2,1)S(1)} %copy-done, s32[1024]{0:T(1024)S(1)} %pad_clamp_fusion), kind=kCustom, calls=%fused_computation | custom fusion | bytes 5242944 | tf_op jit(solution)/shard_map/gather | solution.py:48
  10.7 3.6 %copy.37 = bf16[2,8,128,640]{3,2,0,1:T(8,128)(2,1)} copy(bf16[2,8,128,640]{3,2,1,0:T(8,128)(2,1)} %bitcast.86) | data formatting | bytes 5242880 | tf_op jit(solution)/shard_map/gather | solution.py:48
  14.3 5.3 %all-to-all-start = ((bf16[2,8,128,640]{3,2,0,1:T(8,128)(2,1)}), bf16[2,8,128,640]{3,2,0,1:T(8,128)(2,1)}, u32[]{:S(2)}, u32[]{:S(2)}) async-start(bf16[2,8,128,640]{3,2,0,1:T(8,128)(2,1)} %copy.37), calls=%async_computation | async-start | bytes 5242880 | tf_op jit(solution)/shard_map/all_to_all | solution.py:49
  19.8 2.3 %collective-permute-start = (bf16[4,64,320]{2,0,1:T(4,128)(2,1)S(1)}, bf16[4,64,320]{2,0,1:T(4,128)(2,1)S(1)}, u32[]{:S(2)}, u32[]{:S(2)}) collective-permute-start(bf16[4,64,320]{2,0,1:T(4,128)(2,1)S(1)} %copy.49), channel_id=1, source_target_pairs={{0,1},{1,2},{2,3},{3,0},{4,5},{5,6},{6,7},{7,4},{8,9},{9,10},{10,1... | collective-permute-start | bytes 491528 | tf_op jit(solution)/shard_map/ppermute | solution.py:57
  22.2 2.1 %collective-permute-start.2 = (bf16[4,64,320]{2,0,1:T(4,128)(2,1)S(1)}, bf16[4,64,320]{2,0,1:T(4,128)(2,1)S(1)}, u32[]{:S(2)}, u32[]{:S(2)}) collective-permute-start(bf16[4,64,320]{2,0,1:T(4,128)(2,1)S(1)} %copy.49), channel_id=1, source_target_pairs={{0,3},{1,0},{2,1},{3,2},{4,7},{5,4},{6,5},{7,6},{8,11},{9,8},{10,9... | collective-permute-start | bytes 491528 | tf_op jit(solution)/shard_map/ppermute | solution.py:59
  24.3 5.6 %collective-permute-done = bf16[4,64,320]{2,0,1:T(4,128)(2,1)S(1)} collective-permute-done((bf16[4,64,320]{2,0,1:T(4,128)(2,1)S(1)}, bf16[4,64,320]{2,0,1:T(4,128)(2,1)S(1)}, u32[]{:S(2)}, u32[]{:S(2)}) %collective-permute-start) | collective-permute-done | bytes 163872 | tf_op jit(solution)/shard_map/ppermute | solution.py:57
  30.0 1.6 %copy.55 = bf16[2,1024,320]{2,1,0:T(8,128)(2,1)} copy(bf16[2,1024,320]{1,2,0:T(8,128)(2,1)S(1)} %copy-done.8) | data formatting | bytes 2621440 | tf_op jit(solution)/shard_map/concatenate | solution.py:71
  33.1 11.7 %all-reduce.1 = s32[16]{0:T(128)S(1)} all-reduce(s32[16]{0:T(128)S(1)} %dynamic-update-slice), channel_id=1, replica_groups=mesh['batch'=8,'lib'=4] {'lib'}, use_global_device_ids=true, to_apply=%add.1 | all-reduce | flops 16 | bytes 128
  44.8 2.0 %concatenate.38 = bf16[32,64,320]{2,0,1:T(8,128)(2,1)S(1)} concatenate(bf16[4,64,320]{2,0,1:T(4,128)(2,1)S(1)} %collective-permute-done.1, bf16[4,64,320]{2,0,1:T(4,128)(2,1)S(1)} %collective-permute-done, bf16[4,64,320]{2,0,1:T(4,128)(2,1)S(1)} %copy.49, bf16[4,64,320]{2,0,1:T(4,128)(2,1)S(1)} %collective-permute-done.2, bf16[4,64,320]{2,0,1:T(4,128)(2,1)S(1)} %collective-permute-done.1, ...), dimensions={0} | concatenate | bytes 2621440 | tf_op jit(solution)/shard_map/jit(_roll_dynamic)/concatenate | solution.py:61
  47.1 4.8 %all-to-all-done = bf16[2,8,128,640]{3,2,0,1:T(8,128)(2,1)} async-done(((bf16[2,8,128,640]{3,2,0,1:T(8,128)(2,1)}), bf16[2,8,128,640]{3,2,0,1:T(8,128)(2,1)}, u32[]{:S(2)}, u32[]{:S(2)}) %all-to-all-start) | async-done | bytes 2621472 | tf_op jit(solution)/shard_map/all_to_all | solution.py:49
  52.0 2.1 %copy.38 = bf16[2,8,128,640]{3,2,1,0:T(8,128)(2,1)S(1)} copy(bf16[2,8,128,640]{3,2,0,1:T(8,128)(2,1)} %all-to-all-done) | data formatting | bytes 5242880 | tf_op jit(solution)/shard_map/all_to_all | solution.py:49
  54.1 3.4 %convert_reduce_fusion = f32[2,960]{1,0:T(2,128)S(1)} fusion(bf16[2,1024,640]{2,1,0:T(8,128)(2,1)S(1)} %bitcast.72, bf16[2,1024,320]{2,1,0:T(8,128)(2,1)} %copy.55), kind=kLoop, calls=%fused_computation.3 | loop fusion | flops 9828480 | bytes 3939840 | tf_op jit(solution)/shard_map/reduce_sum | solution.py:17
  57.9 3.6 %fusion.2 = f32[2,960]{1,0:T(2,128)S(1)} fusion(f32[2,960]{1,0:T(2,128)S(1)} %sub.39, bf16[2,1024,640]{2,1,0:T(8,128)(2,1)S(1)} %bitcast.73, bf16[2,1024,320]{2,1,0:T(8,128)(2,1)} %copy.55), kind=kLoop, calls=%fused_computation.6 | loop fusion | flops 13760640 | bytes 3947520 | tf_op jit(solution)/shard_map/reduce_sum | solution.py:18
  62.0 6.8 %multiply_convert_fusion = bf16[2,1024,960]{2,1,0:T(8,128)(2,1)} fusion(f32[960]{0:T(1024)S(1)} %copy-done.10, f32[960]{0:T(1024)S(1)} %copy-done.11, f32[2,960]{1,0:T(2,128)S(1)} %div.50, f32[2,960]{1,0:T(2,128)S(1)} %sub.39, bf16[2,1024,640]{2,1,0:T(8,128)(2,1)S(1)} %bitcast.74, bf16[2,1024,320]{2,1,0:T(8,128)(2,1)} %copy.55), kind=kLoop, calls=%fused_computation.9 | loop fusion | flops 25559040 | bytes 7887360 | tf_op jit(solution)/shard_map/convert_element_type | solution.py:22
  68.8 5.6 %multiply_convert_fusion.1 = bf16[2,32,32,960]{3,2,1,0:T(8,128)(2,1)} fusion(bf16[2,32,32,640]{3,2,1,0:T(8,128)(2,1)S(1)} %bitcast.75, bf16[2,32,32,320]{3,2,1,0:T(8,128)(2,1)S(1)} %bitcast.77, f32[960]{0:T(1024)S(1)} %copy-done.10, f32[960]{0:T(1024)S(1)} %copy-done.11, f32[2,960]{1,0:T(2,128)S(1)} %div.50, f32[2,960]{1,0:T(2,128)S(1)} %sub.39), kind=kLoop, calls=%fused_computation.10 | loop fusion | flops 25559040 | bytes 7887360 | tf_op jit(solution)/shard_map/convert_element_type | solution.py:22
  74.4 22.5 %pad_slice_fusion = (bf16[2,32,32,960]{3,2,1,0:T(8,128)(2,1)S(1)}, bf16[2,32,32,960]{3,2,1,0:T(8,128)(2,1)}, bf16[2,32,32,960]{3,2,1,0:T(8,128)(2,1)}, bf16[2,32...) fusion(bf16[2,32,32,960]{3,2,1,0:T(8,128)(2,1)} %multiply_conve, ...), kind=kLoop, calls=%fused_computation.11 | loop fusion | bytes 35389440 | tf_op jit(solution)/shard_map/slice | solution.py:79
  97.0 4.0 %fusion.30 = f32[2048,320]{0,1:T(8,128)S(1)} fusion(bf16[2048,960]{1,0:T(8,128)(2,1)} %bitcast.88, bf16[3,3,960,320]{2,3,1,0:T(8,128)(2,1)} %param.19), kind=kOutput, calls=%fused_computation.51 | convolution fusion | flops 1258291200 | bytes 7471104 | tf_op jit(solution)/shard_map/dot_general | solution.py:82
  101.0 2.8 %convolution_add_fusion.6 = f32[2048,320]{0,1:T(8,128)S(1)} fusion(f32[2048,320]{0,1:T(8,128)S(1)} %fusion.30, bf16[2048,960]{1,0:T(8,128)(2,1)S(1)} %bitcast.84, bf16[3,3,960,320]{2,3,1,0:T(8,128)(2,1)} %param.19), kind=kOutput, calls=%fused_computation.32 | convolution fusion | flops 1258946560 | bytes 9830400 | tf_op jit(solution)/shard_map/dot_general | solution.py:82
  104.1 1.6 %convolution_add_fusion.5 = f32[2048,320]{0,1:T(8,128)S(1)} fusion(f32[2048,320]{0,1:T(8,128)S(1)} %convolution_add_fusion.6, bf16[2048,960]{1,0:T(8,128)(2,1)S(1)} %bitcast.83, bf16[3,3,960,320]{2,3,1,0:T(8,128)(2,1)S(1)} %bitcast.90), kind=kOutput, calls=%fused_computation.31 | convolution fusion | flops 1258946560 | bytes 10092544 | tf_op jit(solution)/shard_map/dot_general | solution.py:82
  105.7 0.6 copy-done.3
  106.3 1.6 %convolution_add_fusion.4 = f32[2048,320]{0,1:T(8,128)S(1)} fusion(f32[2048,320]{0,1:T(8,128)S(1)} %convolution_add_fusion.5, bf16[2048,960]{1,0:T(8,128)(2,1)S(1)} %bitcast.82, bf16[3,3,960,320]{2,3,1,0:T(8,128)(2,1)S(1)} %bitcast.90), kind=kOutput, calls=%fused_computation.30 | convolution fusion | flops 1258946560 | bytes 10092544 | tf_op jit(solution)/shard_map/dot_general | solution.py:82
  107.8 0.6 copy-done.7
  108.5 3.1 %fusion.24 = f32[2048,320]{0,1:T(8,128)} fusion(bf16[2048,960]{1,0:T(8,128)(2,1)S(1)} %bitcast.87, bf16[3,3,960,320]{2,3,1,0:T(8,128)(2,1)S(1)} %bitcast.90), kind=kOutput, calls=%fused_computation.45 | convolution fusion | flops 1258291200 | bytes 7471104 | tf_op jit(solution)/shard_map/dot_general | solution.py:82
  111.6 3.5 %fusion.12 = f32[2048,320]{0,1:T(8,128)S(1)} fusion(f32[2048,320]{0,1:T(8,128)} %fusion.24, f32[2048,320]{0,1:T(8,128)S(1)} %convolution_add_fusion.4, bf16[2048,960]{1,0:T(8,128)(2,1)S(1)} %bitcast.85, bf16[3,3,960,320]{2,3,1,0:T(8,128)(2,1)S(1)} %bitcast.90), kind=kOutput, calls=%fused_computation.26 | convolution fusion | flops 1259601920 | bytes 12713984 | tf_op jit(solution)/shard_map/dot_general | solution.py:82
  115.0 1.6 %convolution_add_fusion.3 = f32[2048,320]{0,1:T(8,128)S(1)} fusion(f32[2048,320]{0,1:T(8,128)S(1)} %fusion.12, bf16[2048,960]{1,0:T(8,128)(2,1)S(1)} %bitcast.81, bf16[3,3,960,320]{2,3,1,0:T(8,128)(2,1)S(1)} %bitcast.90), kind=kOutput, calls=%fused_computation.29 | convolution fusion | flops 1258946560 | bytes 10092544 | tf_op jit(solution)/shard_map/dot_general | solution.py:82
  116.7 1.6 %convolution_add_fusion.2 = f32[2048,320]{0,1:T(8,128)S(1)} fusion(f32[2048,320]{0,1:T(8,128)S(1)} %convolution_add_fusion.3, bf16[2048,960]{1,0:T(8,128)(2,1)S(1)} %bitcast.80, bf16[3,3,960,320]{2,3,1,0:T(8,128)(2,1)S(1)} %bitcast.90), kind=kOutput, calls=%fused_computation.28 | convolution fusion | flops 1258946560 | bytes 10092544 | tf_op jit(solution)/shard_map/dot_general | solution.py:82
  118.3 1.9 %convolution_add_fusion.1 = f32[2048,320]{0,1:T(8,128)S(1)} fusion(f32[2048,320]{0,1:T(8,128)S(1)} %convolution_add_fusion.2, bf16[2048,960]{1,0:T(8,128)(2,1)S(1)} %bitcast.79, bf16[3,3,960,320]{2,3,1,0:T(8,128)(2,1)S(1)} %bitcast.90), kind=kOutput, calls=%fused_computation.27 | convolution fusion | flops 1258946560 | bytes 10092544 | tf_op jit(solution)/shard_map/dot_general | solution.py:82
  120.2 3.3 %fusion.9 = f32[2048,320]{0,1:T(8,128)} fusion(f32[2048,320]{0,1:T(8,128)S(1)} %convolution_add_fusion.1, bf16[960,320]{0,1:T(8,128)(2,1)S(1)} %copy-done.14, bf16[2048,640]{1,0:T(8,128)(2,1)S(1)} %bitcast.76, bf16[2048,320]{1,0:T(8,128)(2,1)S(1)} %bitcast.78), kind=kOutput, calls=%fused_computation.24 | convolution fusion | flops 1266810880 | bytes 9789440 | tf_op jit(solution)/shard_map/dot_general | solution.py:85
  123.5 2.9 %fusion.17 = bf16[2,64,960]{2,0,1:T(2,128)(2,1)S(1)} fusion(bf16[16,64,960]{2,1,0:T(8,128)(2,1)} %all-gather.2.cloned.1.call-done, s32[16]{0:T(128)S(1)} %all-reduce.1, s32[2]{0:T(128)S(1)} %copy-done.13), kind=kOutput, calls=%fused_computation.39 | convolution fusion | flops 4055072 | bytes 2211912 | tf_op jit(solution)/shard_map/rk,kij->rij/dot_general | solution.py:66
  126.4 6.0 %fusion.14 = bf16[2,1024,320]{1,2,0:T(8,128)(2,1)} fusion(f32[40,2,8,1024]{3,2,1,0:T(8,128)} %bitcast.91, f32[320]{0:T(512)S(1)} %copy-done.12, bf16[2,1024,960]{2,1,0:T(8,128)(2,1)} %multiply_convert_fusion, bf16[2,64,960]{2,0,1:T(2,128)(2,1)S(1)} %fusion.17, bf16[2,64,320]{2,0,1:T(2,128)(2,1)S(1)} %convolution_convert_fusion.1), kind=kOutput, calls=%fused_computation.35 | convolution fusion | flops 337641472 | bytes 8193280 | tf_op jit(solution)/shard_map/rpk,rko->rpo/dot_general | solution.py:93
  (64 shorter events, 2.8 us)
Async XLA Ops:
  6.5 1.8 %copy-start = (bf16[16,128,640]{2,1,0:T(8,128)(2,1)S(1)}, bf16[16,128,640]{2,1,0:T(8,128)(2,1)}, u32[]{:S(2)}) copy-start(bf16[16,128,640]{2,1,0:T(8,128)(2,1)} %param.13) | copy-start | bytes 7864324
  10.7 9.0 %copy-start.9 = (bf16[4,64,320]{2,1,0:T(8,128)(2,1)S(1)}, bf16[4,64,320]{2,1,0:T(8,128)(2,1)}, u32[]{:S(2)}) copy-start(bf16[4,64,320]{2,1,0:T(8,128)(2,1)} %param.18) | copy-start | bytes 491524
  14.3 15.7 %copy-start.8 = (bf16[2,1024,320]{1,2,0:T(8,128)(2,1)S(1)}, bf16[2,1024,320]{1,2,0:T(8,128)(2,1)}, u32[]{:S(2)}) copy-start(bf16[2,1024,320]{1,2,0:T(8,128)(2,1)} %param.12) | copy-start | bytes 3932164
  14.3 17.3 %copy-start.16 = (u32[32]{0:T(128)S(1)}, u32[32]{0:T(128)}, u32[]{:S(2)}) copy-start(u32[32]{0:T(128)} %constant.56) | copy-start | bytes 388
  14.3 18.5 %copy-start.15 = (s32[4]{0:T(128)S(1)}, s32[4]{0:T(128)}, u32[]{:S(2)}) copy-start(s32[4]{0:T(128)} %param.16) | copy-start | bytes 52
  14.3 37.7 %all-to-all-start = ((bf16[2,8,128,640]{3,2,0,1:T(8,128)(2,1)}), bf16[2,8,128,640]{3,2,0,1:T(8,128)(2,1)}, u32[]{:S(2)}, u32[]{:S(2)}) async-start(bf16[2,8,128,640]{3,2,0,1:T(8,128)(2,1)} %copy.37), calls=%async_computation | async-start | bytes 5242880 | tf_op jit(solution)/shard_map/all_to_all | solution.py:49
  19.6 27.2 %copy-start.13 = (s32[2]{0:T(128)S(1)}, s32[2]{0:T(128)}, u32[]{:S(2)}) copy-start(s32[2]{0:T(128)} %param.15) | copy-start | bytes 28
  19.6 103.9 %all-gather.2.cloned.1.call-start = ((), (), s32[]{:S(2)}) async-start(), calls=%async_computation.1 | async-start | bytes 2621440 | tf_op jit(solution)/shard_map/all_gather | solution.py:51
  19.8 10.1 %collective-permute-start = (bf16[4,64,320]{2,0,1:T(4,128)(2,1)S(1)}, bf16[4,64,320]{2,0,1:T(4,128)(2,1)S(1)}, u32[]{:S(2)}, u32[]{:S(2)}) collective-permute-start(bf16[4,64,320]{2,0,1:T(4,128)(2,1)S(1)} %copy.49), channel_id=1, source_target_pairs={{0,1},{1,2},{2,3},{3,0},{4,5},{5,6},{6,7},{7,4},{8,9},{9,10},{10,1... | collective-permute-start | bytes 491528 | tf_op jit(solution)/shard_map/ppermute | solution.py:57
  22.2 22.6 %collective-permute-start.2 = (bf16[4,64,320]{2,0,1:T(4,128)(2,1)S(1)}, bf16[4,64,320]{2,0,1:T(4,128)(2,1)S(1)}, u32[]{:S(2)}, u32[]{:S(2)}) collective-permute-start(bf16[4,64,320]{2,0,1:T(4,128)(2,1)S(1)} %copy.49), channel_id=1, source_target_pairs={{0,3},{1,0},{2,1},{3,2},{4,7},{5,4},{6,5},{7,6},{8,11},{9,8},{10,9... | collective-permute-start | bytes 491528 | tf_op jit(solution)/shard_map/ppermute | solution.py:59
  29.9 14.9 %collective-permute-start.1 = (bf16[4,64,320]{2,0,1:T(4,128)(2,1)S(1)}, bf16[4,64,320]{2,0,1:T(4,128)(2,1)S(1)}, u32[]{:S(2)}, u32[]{:S(2)}) collective-permute-start(bf16[4,64,320]{2,0,1:T(4,128)(2,1)S(1)} %collective-permute-done), channel_id=1, source_target_pairs={{0,1},{1,2},{2,3},{3,0},{4,5},{5,6},{6,7},{7,4},{8,9},{9,10},{10,1... | collective-permute-start | bytes 491528 | tf_op jit(solution)/shard_map/ppermute | solution.py:57
  54.1 7.9 %copy-start.10 = (f32[960]{0:T(1024)S(1)}, f32[960]{0:T(1024)}, u32[]{:S(2)}) copy-start(f32[960]{0:T(1024)} %param.22) | copy-start | bytes 11524
  54.1 7.9 %copy-start.11 = (f32[960]{0:T(1024)S(1)}, f32[960]{0:T(1024)}, u32[]{:S(2)}) copy-start(f32[960]{0:T(1024)} %param.21) | copy-start | bytes 11524
  62.0 6.9 %copy-start.2 = (bf16[2,1024,320]{2,1,0:T(8,128)(2,1)S(1)}, bf16[2,1024,320]{2,1,0:T(8,128)(2,1)}, u32[]{:S(2)}) copy-start(bf16[2,1024,320]{2,1,0:T(8,128)(2,1)} %copy.55) | copy-start | bytes 3932164
  96.9 4.1 %copy-start.5 = (bf16[2,32,32,960]{3,2,1,0:T(8,128)(2,1)S(1)}, bf16[2,32,32,960]{3,2,1,0:T(8,128)(2,1)}, u32[]{:S(2)}) copy-start(bf16[2,32,32,960]{3,2,1,0:T(8,128)(2,1)} %get-tuple-element.6) | copy-start | bytes 11796484
  96.9 6.9 %slice-start = ((s8[5898240]{0:T(1024)(128)(4,1)}), s8[4194304]{0:T(1024)(128)(4,1)S(1)}, s32[]{:S(2)}) async-start(s8[5898240]{0:T(1024)(128)(4,1)} %bitcast.89), calls=%async_computation.2 | async-start | bytes 8388608
  101.0 2.9 %copy-start.4 = (bf16[2,32,32,960]{3,2,1,0:T(8,128)(2,1)S(1)}, bf16[2,32,32,960]{3,2,1,0:T(8,128)(2,1)}, u32[]{:S(2)}) copy-start(bf16[2,32,32,960]{3,2,1,0:T(8,128)(2,1)} %get-tuple-element.7) | copy-start | bytes 11796484
  101.0 3.0 %slice-start.1 = ((s8[5898240]{0:T(1024)(128)(4,1)}), s8[1703936]{0:T(1024)(128)(4,1)S(1)}, s32[]{:S(2)}) async-start(s8[5898240]{0:T(1024)(128)(4,1)} %bitcast.89), calls=%async_computation.3 | async-start | bytes 3407872
  104.1 2.2 %copy-start.3 = (bf16[2,32,32,960]{3,2,1,0:T(8,128)(2,1)S(1)}, bf16[2,32,32,960]{3,2,1,0:T(8,128)(2,1)}, u32[]{:S(2)}) copy-start(bf16[2,32,32,960]{3,2,1,0:T(8,128)(2,1)} %get-tuple-element.8) | copy-start | bytes 11796484
  106.3 2.2 %copy-start.7 = (bf16[2,32,32,960]{3,2,1,0:T(8,128)(2,1)S(1)}, bf16[2,32,32,960]{3,2,1,0:T(8,128)(2,1)}, u32[]{:S(2)}) copy-start(bf16[2,32,32,960]{3,2,1,0:T(8,128)(2,1)} %get-tuple-element.9) | copy-start | bytes 11796484
  108.5 3.1 %copy-start.6 = (bf16[2,1024,960]{2,1,0:T(8,128)(2,1)S(1)}, bf16[2,1024,960]{2,1,0:T(8,128)(2,1)}, u32[]{:S(2)}) copy-start(bf16[2,1024,960]{2,1,0:T(8,128)(2,1)} %multiply_convert_fusion) | copy-start | bytes 11796484
  118.3 1.9 %copy-start.14 = (bf16[960,320]{0,1:T(8,128)(2,1)S(1)}, bf16[960,320]{0,1:T(8,128)(2,1)}, u32[]{:S(2)}) copy-start(bf16[960,320]{0,1:T(8,128)(2,1)} %param.20) | copy-start | bytes 1843204
  120.2 6.2 %copy-start.12 = (f32[320]{0:T(512)S(1)}, f32[320]{0:T(512)}, u32[]{:S(2)}) copy-start(f32[320]{0:T(512)} %param.23) | copy-start | bytes 3844
  126.4 6.0 %copy-start.1 = (bf16[16,128,640]{2,1,0:T(8,128)(2,1)S(1)}, bf16[16,128,640]{2,1,0:T(8,128)(2,1)}, u32[]{:S(2)}) copy-start(bf16[16,128,640]{2,1,0:T(8,128)(2,1)} %param.13) | copy-start | bytes 7864324
Sparse Core Ops, SparseCore 0:
  30.1 49.3 all-gather.1
